TPU v7x, 32 devices: a whole 2x2x4 slice. The times are simulated.
32 devices in a mesh: row: 16 (over z, y, core), col: 2 (over x).
Axes of the slice: x: 2, y: 2, z: 4, core: 2. Of those that a mesh axis runs over, the one named last changes fastest.
Arguments:
- currents: float32 [8, 131072], P(None, ('row', 'col')), may hold values from -6 to 6
- src_pos: float32 [3, 131072], P(None, ('row', 'col')), may hold values from 0 to 1
- src_dir: float32 [3, 131072], P(None, ('row', 'col')), may hold values from -1 to 1
- cell_ends: int32 [2, 131072], P(None, ('row', 'col')), may hold values from 0 to 65535, as said below
- pan_pos: float32 [3, 65536], P(None, ('row', 'col')), may hold values from 0 to 1
- tgt_pos: float32 [3, 4096], P(None, 'row'), may hold values from 0 to 1
- tgt_dir: float32 [3, 4096], P(None, 'row'), may hold values from -1 to 1
- tgt_ends: int32 [2, 4096], P(None, 'row'), may hold values from 0 to 2047, as said below
- wpan_pos: float32 [3, 2048], P(None, 'row'), may hold values from 0 to 1
Outputs:
- voltage: float32 [8, 4096], P(None, ('row', 'col'))
Inputs may be any that keep to these rules, and one draw needn't show every extreme that they name: `cell_ends`: A cell's two panels differ. Source cell j and its panels belong to devices with the same col index: with b = j // 4096 and c = p // 2048, b and c leave the same remainder on division by 2. `tgt_ends`: A target cell's two panels differ.
All inputs are finite; a program needn't handle non-finite values.
Results may differ from a plain program's by a relative error of at most 0.006.
Values may be sent and summed in bfloat16 or wider, within the bound.
A program may use at most 192 MiB of HBM per device.

v0:
```python
import math

import jax
import jax.numpy as jnp
from jax import lax
from jax.sharding import PartitionSpec as P

CELLS = 131072
PANELS = 65536


soft_sq = 0.0004
wave_num = 12.0


def kernel_tile(tpos, spos, tdir, sdir):
    dx = tpos[0][:, None] - spos[0][None, :]
    dy = tpos[1][:, None] - spos[1][None, :]
    dz = tpos[2][:, None] - spos[2][None, :]
    dist_sq = dx * dx + dy * dy + dz * dz + soft_sq
    inverse = lax.rsqrt(dist_sq)
    phase = wave_num * dist_sq * inverse
    real_part = jnp.cos(phase) * inverse
    imag_part = -jnp.sin(phase) * inverse
    if tdir is not None:
        inner = (
            tdir[0][:, None] * sdir[0][None, :]
            + tdir[1][:, None] * sdir[1][None, :]
            + tdir[2][:, None] * sdir[2][None, :]
        )
        real_part = real_part * inner
        imag_part = imag_part * inner
    return jnp.concatenate([real_part, imag_part], axis=1).astype(jnp.bfloat16)


def apply_tile(stacked, source):
    half = source.shape[0] // 2
    real_src = source[:half]
    imag_src = source[half:]
    left = jnp.concatenate(
        [jnp.concatenate([real_src, -imag_src], 1), jnp.concatenate([imag_src, real_src], 1)], 0
    )
    return lax.dot_general(
        left, stacked, (((1,), (1,)), ((), ())), preferred_element_type=jnp.float32
    )


def sweep(tpos, tdir, spos, sdir, source):
    length = spos.shape[1]
    width = min(length, 2048)
    total = None
    for block in range(length // width):
        lower = block * width
        upper = lower + width
        sub_dir = None if sdir is None else sdir[:, lower:upper]
        term = apply_tile(
            kernel_tile(tpos, spos[:, lower:upper], tdir, sub_dir), source[:, lower:upper]
        )
        total = term if total is None else total + term
    return total


def per_device(
    currents, src_pos, src_dir, cell_ends, pan_pos, tgt_pos, tgt_dir, tgt_ends, wpan_pos
):
    doubled = currents.shape[0]
    half = doubled // 2
    col_count = lax.axis_size("col")
    col_index = lax.axis_index("col")
    panel_dev = pan_pos.shape[1]
    block_len = panel_dev * lax.axis_size("row")
    cur16 = currents.astype(jnp.bfloat16)
    cur_all = lax.all_gather(cur16, "row", axis=1, tiled=True)
    charge_zero = jnp.zeros((doubled, block_len), jnp.float32)
    spos = lax.all_gather(src_pos, "row", axis=1, tiled=True)
    sdir = lax.all_gather(src_dir, "row", axis=1, tiled=True)
    source = cur_all
    induct = sweep(tgt_pos, tgt_dir, spos, sdir, source)
    cur_wide = cur16.astype(jnp.float32)
    local_ends = cell_ends // (panel_dev * col_count) * panel_dev + cell_ends % panel_dev
    partial_value = (
        charge_zero.at[:, local_ends[0]].add(cur_wide).at[:, local_ends[1]].add(-cur_wide)
    )
    q_piece = lax.psum_scatter(partial_value, "row", scatter_dimension=1, tiled=True)
    source = lax.all_gather(q_piece, "row", axis=1, tiled=True)
    ppos = lax.all_gather(pan_pos, "row", axis=1, tiled=True)
    field = sweep(wpan_pos, None, ppos, None, source.astype(jnp.bfloat16))
    share = tgt_pos.shape[1] // col_count
    induct_all, field_all = lax.psum((induct, field), "col")
    induct_mine = lax.dynamic_slice_in_dim(induct_all, col_index * share, share, 1)
    pscale = 0.25 / math.sqrt(PANELS)
    lscale = 1.0 / math.sqrt(CELLS)
    potential_part = jnp.concatenate([field_all[half:], -field_all[:half]], 0) * pscale
    potential = lax.all_gather(potential_part, "row", axis=1, tiled=True)
    voltage = jnp.concatenate([-induct_mine[half:], induct_mine[:half]], 0) * lscale
    my_ends = lax.dynamic_slice_in_dim(tgt_ends, col_index * share, share, 1)
    return (
        voltage + jnp.take(potential, my_ends[0], axis=1) - jnp.take(potential, my_ends[1], axis=1)
    )


def solution(mesh):
    return jax.shard_map(
        per_device,
        mesh=mesh,
        in_specs=(
            P(None, ("row", "col")),
            P(None, ("row", "col")),
            P(None, ("row", "col")),
            P(None, ("row", "col")),
            P(None, ("row", "col")),
            P(None, "row"),
            P(None, "row"),
            P(None, "row"),
            P(None, "row"),
        ),
        out_specs=P(None, ("row", "col")),
        check_vma=False,
    )
```

profile of v0, /device:TPU:0, one launch (start us, length us, event | category | flops | bytes accessed | tf_op | source)
XLA Modules:
  0.0 625.1 jit_solution(3184239134539775708)
XLA Ops:
  6.5 0.9 fusion.272
  7.5 0.9 fusion.609
  8.5 1.9 copy.92
  11.0 29.5 %scatter_custom_fusion = f32[8,32768]{0,1:T(8,128)} fusion(s32[4096]{0:T(1024)S(1)} %bitcast.277, f32[4096,8]{1,0:T(8,128)} %copy.92, f32[]{:T(128)} %constant.56.clone.1), kind=kCustom, calls=%fused_computation.4 | custom fusion | flops 32768 | bytes 1049088 | tf_op jit(solution)/shard_map/scatter-add | solution.py:82
  40.5 31.7 %scatter_fusion = f32[8,32768]{0,1:T(8,128)} fusion(f32[8,32768]{0,1:T(8,128)} %scatter_custom_fusion, s32[4096]{0:T(1024)S(1)} %bitcast.276, f32[4096,8]{1,0:T(8,128)S(1)} %copy.93), kind=kCustom, calls=%fused_computation.3 | custom fusion | flops 32768 | bytes 409600 | tf_op jit(solution)/shard_map/scatter-add | solution.py:82
  72.2 9.8 %copy.94 = f32[8,32768]{1,0:T(8,128)} copy(f32[8,32768]{0,1:T(8,128)} %scatter_fusion) | data formatting | bytes 2097152 | tf_op jit(solution)/shard_map/scatter-add | solution.py:82
  82.1 0.7 all-gather.3.cloned.1.call-update
  82.9 26.2 %all_gather.20 = f32[3,65536]{1,0:T(4,128)S(1)} all-gather(f32[3,4096]{1,0:T(4,128)S(1)} %copy-done.4), channel_id=1, replica_groups=mesh['row'=16,'col'=2] {'row'}, dimensions={1}, use_global_device_ids=true | all-gather | bytes 835584 | tf_op jit(solution)/shard_map/all_gather | solution.py:76
  109.4 22.9 %all_gather.19 = f32[3,65536]{1,0:T(4,128)S(1)} all-gather(f32[3,4096]{1,0:T(4,128)S(1)} %copy-done.5), channel_id=1, replica_groups=mesh['row'=16,'col'=2] {'row'}, dimensions={1}, use_global_device_ids=true | all-gather | bytes 835584 | tf_op jit(solution)/shard_map/all_gather | solution.py:75
  133.3 20.3 %all_gather.22 = f32[3,32768]{1,0:T(4,128)S(1)} all-gather(f32[3,2048]{1,0:T(4,128)S(1)} %copy-done.6), channel_id=1, replica_groups=mesh['row'=16,'col'=2] {'row'}, dimensions={1}, use_global_device_ids=true | all-gather | bytes 417792 | tf_op jit(solution)/shard_map/all_gather | solution.py:86
  154.0 19.4 %multiply_convert_fusion.31 = (bf16[256,2048]{1,0:T(8,128)(2,1)}, bf16[256,2048]{1,0:T(8,128)(2,1)}, bf16[256,2048]{1,0:T(8,128)(2,1)}, bf16[256,2048]{1,0:T(8,128)(2,1)}) fusion(f32[2048]{0:T(1024)S(1)} %bitcast.431, f32[2048]{0:T(1024)S(1)} %bitcast.432, f32[2048]{0:T(1024)S(1)} %bitcast.433, f32[2048]{0:T(1024)S(1)} %bitcast.488, f32[2048]{0:T(1024)S(1)} %bitcast.489, ...), kind=kLoop, calls=%fused_computation.210 | loop fusion | flops 24117248 | bytes 4298752 | tf_op jit(solution)/shard_map/convert.62
  173.4 19.2 %multiply_convert_fusion.1 = (bf16[256,2048]{1,0:T(8,128)(2,1)}, bf16[256,2048]{1,0:T(8,128)(2,1)}, bf16[256,2048]{1,0:T(8,128)(2,1)}, bf16[256,2048]{1,0:T(8,128)(2,1)}) fusion(f32[2048]{0:T(1024)S(1)} %bitcast.508, f32[2048]{0:T(1024)S(1)} %bitcast.509, f32[2048]{0:T(1024)S(1)} %bitcast.507, f32[2048]{0:T(1024)S(1)} %bitcast.514, f32[2048]{0:T(1024)S(1)} %bitcast.515, ...), kind=kLoop, calls=%fused_computation.135 | loop fusion | flops 24117248 | bytes 4298752 | tf_op jit(solution)/shard_map/convert.32
  192.6 19.5 %multiply_convert_fusion.3 = (bf16[256,2048]{1,0:T(8,128)(2,1)}, bf16[256,2048]{1,0:T(8,128)(2,1)}, bf16[256,2048]{1,0:T(8,128)(2,1)}, bf16[256,2048]{1,0:T(8,128)(2,1)}) fusion(f32[2048]{0:T(1024)S(1)} %bitcast.497, f32[2048]{0:T(1024)S(1)} %bitcast.498, f32[2048]{0:T(1024)S(1)} %bitcast.499, f32[2048]{0:T(1024)S(1)} %bitcast.510, f32[2048]{0:T(1024)S(1)} %bitcast.511, ...), kind=kLoop, calls=%fused_computation.140 | loop fusion | flops 24117248 | bytes 4298752 | tf_op jit(solution)/shard_map/convert.34
  212.1 19.3 %multiply_convert_fusion.5 = (bf16[256,2048]{1,0:T(8,128)(2,1)}, bf16[256,2048]{1,0:T(8,128)(2,1)}, bf16[256,2048]{1,0:T(8,128)(2,1)}, bf16[256,2048]{1,0:T(8,128)(2,1)}) fusion(f32[2048]{0:T(1024)S(1)} %bitcast.480, f32[2048]{0:T(1024)S(1)} %bitcast.481, f32[2048]{0:T(1024)S(1)} %bitcast.482, f32[2048]{0:T(1024)S(1)} %bitcast.500, f32[2048]{0:T(1024)S(1)} %bitcast.501, ...), kind=kLoop, calls=%fused_computation.145 | loop fusion | flops 24117248 | bytes 4298752 | tf_op jit(solution)/shard_map/convert.36
  231.4 19.7 %multiply_convert_fusion.7 = (bf16[256,2048]{1,0:T(8,128)(2,1)}, bf16[256,2048]{1,0:T(8,128)(2,1)}, bf16[256,2048]{1,0:T(8,128)(2,1)}, bf16[256,2048]{1,0:T(8,128)(2,1)}) fusion(f32[2048]{0:T(1024)S(1)} %bitcast.464, f32[2048]{0:T(1024)S(1)} %bitcast.465, f32[2048]{0:T(1024)S(1)} %bitcast.466, f32[2048]{0:T(1024)S(1)} %bitcast.485, f32[2048]{0:T(1024)S(1)} %bitcast.486, ...), kind=kLoop, calls=%fused_computation.150 | loop fusion | flops 24117248 | bytes 4298752 | tf_op jit(solution)/shard_map/convert.38
  251.1 19.3 %multiply_convert_fusion.9 = (bf16[256,2048]{1,0:T(8,128)(2,1)}, bf16[256,2048]{1,0:T(8,128)(2,1)}, bf16[256,2048]{1,0:T(8,128)(2,1)}, bf16[256,2048]{1,0:T(8,128)(2,1)}) fusion(f32[2048]{0:T(1024)S(1)} %bitcast.437, f32[2048]{0:T(1024)S(1)} %bitcast.438, f32[2048]{0:T(1024)S(1)} %bitcast.439, f32[2048]{0:T(1024)S(1)} %bitcast.470, f32[2048]{0:T(1024)S(1)} %bitcast.471, ...), kind=kLoop, calls=%fused_computation.155 | loop fusion | flops 24117248 | bytes 4298752 | tf_op jit(solution)/shard_map/convert.40
  270.3 19.5 %multiply_convert_fusion.11 = (bf16[256,2048]{1,0:T(8,128)(2,1)}, bf16[256,2048]{1,0:T(8,128)(2,1)}, bf16[256,2048]{1,0:T(8,128)(2,1)}, bf16[256,2048]{1,0:T(8,128)(2,1)}) fusion(f32[2048]{0:T(1024)S(1)} %bitcast.412, f32[2048]{0:T(1024)S(1)} %bitcast.413, f32[2048]{0:T(1024)S(1)} %bitcast.414, f32[2048]{0:T(1024)S(1)} %bitcast.449, f32[2048]{0:T(1024)S(1)} %bitcast.450, ...), kind=kLoop, calls=%fused_computation.160 | loop fusion | flops 24117248 | bytes 4298752 | tf_op jit(solution)/shard_map/convert.42
  289.8 19.3 %multiply_convert_fusion.13 = (bf16[256,2048]{1,0:T(8,128)(2,1)}, bf16[256,2048]{1,0:T(8,128)(2,1)}, bf16[256,2048]{1,0:T(8,128)(2,1)}, bf16[256,2048]{1,0:T(8,128)(2,1)}) fusion(f32[2048]{0:T(1024)S(1)} %bitcast.402, f32[2048]{0:T(1024)S(1)} %bitcast.484, f32[2048]{0:T(1024)S(1)} %bitcast.483, f32[2048]{0:T(1024)S(1)} %bitcast.427, f32[2048]{0:T(1024)S(1)} %bitcast.504, ...), kind=kLoop, calls=%fused_computation.165 | loop fusion | flops 24117248 | bytes 4298752 | tf_op jit(solution)/shard_map/convert.44
  309.0 19.5 %multiply_convert_fusion.15 = (bf16[256,2048]{1,0:T(8,128)(2,1)}, bf16[256,2048]{1,0:T(8,128)(2,1)}, bf16[256,2048]{1,0:T(8,128)(2,1)}, bf16[256,2048]{1,0:T(8,128)(2,1)}) fusion(f32[2048]{0:T(1024)S(1)} %bitcast.467, f32[2048]{0:T(1024)S(1)} %bitcast.468, f32[2048]{0:T(1024)S(1)} %bitcast.469, f32[2048]{0:T(1024)S(1)} %bitcast.491, f32[2048]{0:T(1024)S(1)} %bitcast.492, ...), kind=kLoop, calls=%fused_computation.170 | loop fusion | flops 24117248 | bytes 4298752 | tf_op jit(solution)/shard_map/convert.46
  328.5 19.3 %multiply_convert_fusion.17 = (bf16[256,2048]{1,0:T(8,128)(2,1)}, bf16[256,2048]{1,0:T(8,128)(2,1)}, bf16[256,2048]{1,0:T(8,128)(2,1)}, bf16[256,2048]{1,0:T(8,128)(2,1)}) fusion(f32[2048]{0:T(1024)S(1)} %bitcast.446, f32[2048]{0:T(1024)S(1)} %bitcast.447, f32[2048]{0:T(1024)S(1)} %bitcast.448, f32[2048]{0:T(1024)S(1)} %bitcast.473, f32[2048]{0:T(1024)S(1)} %bitcast.474, ...), kind=kLoop, calls=%fused_computation.175 | loop fusion | flops 24117248 | bytes 4298752 | tf_op jit(solution)/shard_map/convert.48
  347.8 19.7 %multiply_convert_fusion.19 = (bf16[256,2048]{1,0:T(8,128)(2,1)}, bf16[256,2048]{1,0:T(8,128)(2,1)}, bf16[256,2048]{1,0:T(8,128)(2,1)}, bf16[256,2048]{1,0:T(8,128)(2,1)}) fusion(f32[2048]{0:T(1024)S(1)} %bitcast.421, f32[2048]{0:T(1024)S(1)} %bitcast.422, f32[2048]{0:T(1024)S(1)} %bitcast.423, f32[2048]{0:T(1024)S(1)} %bitcast.453, f32[2048]{0:T(1024)S(1)} %bitcast.454, ...), kind=kLoop, calls=%fused_computation.180 | loop fusion | flops 24117248 | bytes 4298752 | tf_op jit(solution)/shard_map/convert.50
  367.5 19.3 %multiply_convert_fusion.21 = (bf16[256,2048]{1,0:T(8,128)(2,1)}, bf16[256,2048]{1,0:T(8,128)(2,1)}, bf16[256,2048]{1,0:T(8,128)(2,1)}, bf16[256,2048]{1,0:T(8,128)(2,1)}) fusion(f32[2048]{0:T(1024)S(1)} %bitcast.399, f32[2048]{0:T(1024)S(1)} %bitcast.400, f32[2048]{0:T(1024)S(1)} %bitcast.401, f32[2048]{0:T(1024)S(1)} %bitcast.424, f32[2048]{0:T(1024)S(1)} %bitcast.425, ...), kind=kLoop, calls=%fused_computation.185 | loop fusion | flops 24117248 | bytes 4298752 | tf_op jit(solution)/shard_map/convert.52
  386.8 19.4 %multiply_convert_fusion.23 = (bf16[256,2048]{1,0:T(8,128)(2,1)}, bf16[256,2048]{1,0:T(8,128)(2,1)}, bf16[256,2048]{1,0:T(8,128)(2,1)}, bf16[256,2048]{1,0:T(8,128)(2,1)}) fusion(f32[2048]{0:T(1024)S(1)} %bitcast.372, f32[2048]{0:T(1024)S(1)} %bitcast.373, f32[2048]{0:T(1024)S(1)} %bitcast.374, f32[2048]{0:T(1024)S(1)} %bitcast.403, f32[2048]{0:T(1024)S(1)} %bitcast.404, ...), kind=kLoop, calls=%fused_computation.190 | loop fusion | flops 24117248 | bytes 4298752 | tf_op jit(solution)/shard_map/convert.54
  406.2 19.3 %multiply_convert_fusion.25 = (bf16[256,2048]{1,0:T(8,128)(2,1)}, bf16[256,2048]{1,0:T(8,128)(2,1)}, bf16[256,2048]{1,0:T(8,128)(2,1)}, bf16[256,2048]{1,0:T(8,128)(2,1)}) fusion(f32[2048]{0:T(1024)S(1)} %bitcast.336, f32[2048]{0:T(1024)S(1)} %bitcast.337, f32[2048]{0:T(1024)S(1)} %bitcast.302, f32[2048]{0:T(1024)S(1)} %bitcast.381, f32[2048]{0:T(1024)S(1)} %bitcast.382, ...), kind=kLoop, calls=%fused_computation.195 | loop fusion | flops 24117248 | bytes 4298752 | tf_op jit(solution)/shard_map/convert.56
  425.5 23.0 %multiply_convert_fusion.65 = (bf16[128,2048]{1,0:T(8,128)(2,1)S(1)}, bf16[128,2048]{1,0:T(8,128)(2,1)S(1)}, bf16[128,2048]{1,0:T(8,128)(2,1)}, bf16[128,2048]{1...) fusion(f32[2048]{0:T(1024)S(1)} %bitcast.355, ...), kind=kLoop, calls=%fused_computation.390 | loop fusion | flops 20971520 | bytes 5367296 | tf_op jit(solution)/shard_map/convert
  448.5 22.7 %multiply_convert_fusion.67 = (bf16[128,2048]{1,0:T(8,128)(2,1)S(1)}, bf16[128,2048]{1,0:T(8,128)(2,1)}, bf16[128,2048]{1,0:T(8,128)(2,1)}, bf16[128,2048]{1,0:T...) fusion(f32[2048]{0:T(1024)S(1)} %bitcast.333, ...), kind=kLoop, calls=%fused_computation.394 | loop fusion | flops 20971520 | bytes 5367296 | tf_op jit(solution)/shard_map/convert.2
  471.1 22.9 %multiply_convert_fusion.69 = (bf16[128,2048]{1,0:T(8,128)(2,1)}, bf16[128,2048]{1,0:T(8,128)(2,1)}, bf16[128,2048]{1,0:T(8,128)(2,1)}, bf16[128,2048]{1,0:T(8,1...) fusion(f32[2048]{0:T(1024)S(1)} %bitcast.313, ...), kind=kLoop, calls=%fused_computation.398 | loop fusion | flops 20971520 | bytes 5367296 | tf_op jit(solution)/shard_map/convert.4
  494.0 4.5 multiply_convert_fusion.95
  498.6 19.3 %multiply_convert_fusion.27 = (bf16[256,2048]{1,0:T(8,128)(2,1)}, bf16[256,2048]{1,0:T(8,128)(2,1)}, bf16[256,2048]{1,0:T(8,128)(2,1)}, bf16[256,2048]{1,0:T(8,128)(2,1)}) fusion(f32[2048]{0:T(1024)S(1)} %bitcast.284, f32[2048]{0:T(1024)S(1)} %bitcast.285, f32[2048]{0:T(1024)S(1)} %bitcast.286, f32[2048]{0:T(1024)S(1)} %bitcast.296, f32[2048]{0:T(1024)S(1)} %bitcast.297, ...), kind=kLoop, calls=%fused_computation.200 | loop fusion | flops 24117248 | bytes 4298752 | tf_op jit(solution)/shard_map/convert.58
  517.9 19.6 %multiply_convert_fusion.29 = (bf16[256,2048]{1,0:T(8,128)(2,1)}, bf16[256,2048]{1,0:T(8,128)(2,1)}, bf16[256,2048]{1,0:T(8,128)(2,1)}, bf16[256,2048]{1,0:T(8,128)(2,1)}) fusion(f32[2048]{0:T(1024)S(1)} %bitcast.278, f32[2048]{0:T(1024)S(1)} %bitcast.279, f32[2048]{0:T(1024)S(1)} %bitcast.280, f32[2048]{0:T(1024)S(1)} %bitcast.290, f32[2048]{0:T(1024)S(1)} %bitcast.291, ...), kind=kLoop, calls=%fused_computation.205 | loop fusion | flops 24117248 | bytes 4298752 | tf_op jit(solution)/shard_map/convert.60
  537.6 0.8 slice.2111
  538.4 1.2 fusion.671
  539.6 1.4 slice_negate_fusion.18
  541.1 2.2 fusion.2
  543.3 0.6 fusion.220
  544.8 0.6 fusion.217
  545.7 0.7 fusion.214
  547.1 0.6 fusion.211
  548.0 0.6 fusion.208
  549.4 0.6 fusion.205
  550.4 0.6 fusion.202
  551.6 0.6 fusion.199
  552.7 0.6 fusion.196
  554.3 0.6 fusion.193
  555.3 0.6 fusion.190
  556.6 0.7 fusion.187
  557.7 0.6 fusion.184
  558.9 0.6 fusion.181
  560.1 0.6 fusion.178
  561.2 0.6 fusion.175
  562.4 0.6 fusion.172
  563.6 0.6 fusion.169
  564.9 0.6 fusion.166
  568.3 0.8 fusion.157
  569.5 0.6 fusion.154
  570.8 0.6 fusion.151
  571.9 0.6 fusion.148
  576.6 0.6 fusion.136
  577.7 0.6 fusion.133
  579.6 1.4 convert_element_type.8
  589.9 8.1 %all-reduce = (f32[8,256]{1,0:T(8,128)S(1)}, f32[8,128]{1,0:T(8,128)S(1)}) all-reduce(f32[8,256]{1,0:T(8,128)S(1)} %fusion.130, f32[8,128]{1,0:T(8,128)S(1)} %convolution_add_fusion), channel_id=1, replica_groups=mesh['row'=16,'col'=2] {'col'}, use_global_device_ids=true, to_apply=%region_0.1 | all-reduce | flops 3072 | bytes 24576 | tf_op jit(solution)/shard_map/psum | solution.py:89
  598.0 18.0 %all_gather.23 = f32[8,2048]{1,0:T(8,128)S(1)} all-gather(f32[8,128]{1,0:T(8,128)S(1)} %maximum_multiply_fusion.1), channel_id=1, replica_groups=mesh['row'=16,'col'=2] {'row'}, dimensions={1}, use_global_device_ids=true | all-gather | bytes 69632 | tf_op jit(solution)/shard_map/all_gather | solution.py:94
  616.4 0.7 gather_fusion.1
  617.1 0.7 gather_fusion
  (266 shorter events, 32.2 us)
Async XLA Ops:
  6.5 147.4 %copy-start = (s32[2,256]{1,0:T(2,128)S(1)}, s32[2,256]{1,0:T(2,128)}, u32[]{:S(2)}) copy-start(s32[2,256]{1,0:T(2,128)} %param.18) | copy-start | bytes 6148
  6.5 531.0 %reduce-scatter.2.cloned.1.call-start = ((), (), s32[]{:S(2)}) async-start(), calls=%async_computation.2 | async-start | bytes 1114112 | tf_op jit(solution)/shard_map/reduce_scatter | solution.py:84
  7.5 3.5 copy-start.3
  72.2 10.6 %copy-start.4 = (f32[3,4096]{1,0:T(4,128)S(1)}, f32[3,4096]{1,0:T(4,128)}, u32[]{:S(2)}) copy-start(f32[3,4096]{1,0:T(4,128)} %param.13) | copy-start | bytes 147460
  82.0 27.3 %copy-start.5 = (f32[3,4096]{1,0:T(4,128)S(1)}, f32[3,4096]{1,0:T(4,128)}, u32[]{:S(2)}) copy-start(f32[3,4096]{1,0:T(4,128)} %param.12) | copy-start | bytes 147460
  82.1 455.6 %all-gather.3.cloned.1.call-start = ((), (), s32[]{:S(2)}) async-start(), calls=%async_computation.1 | async-start | bytes 1114112 | tf_op jit(solution)/shard_map/all_gather | solution.py:73
  82.8 496.7 %all-gather.5.cloned.1.call-start = ((), (), s32[]{:S(2)}) async-start(), calls=%async_computation.3 | async-start | bytes 1114112 | tf_op jit(solution)/shard_map/all_gather | solution.py:85
  109.1 24.1 %copy-start.6 = (f32[3,2048]{1,0:T(4,128)S(1)}, f32[3,2048]{1,0:T(4,128)}, u32[]{:S(2)}) copy-start(f32[3,2048]{1,0:T(4,128)} %param.15) | copy-start | bytes 73732
  132.2 21.6 %copy-start.7 = (f32[3,256]{1,0:T(4,128)S(1)}, f32[3,256]{1,0:T(4,128)}, u32[]{:S(2)}) copy-start(f32[3,256]{1,0:T(4,128)} %param.17) | copy-start | bytes 9220
  132.2 21.6 %copy-start.8 = (f32[3,256]{1,0:T(4,128)S(1)}, f32[3,256]{1,0:T(4,128)}, u32[]{:S(2)}) copy-start(f32[3,256]{1,0:T(4,128)} %param.16) | copy-start | bytes 9220
  132.2 21.7 %copy-start.9 = (f32[3,128]{1,0:T(4,128)S(1)}, f32[3,128]{1,0:T(4,128)}, u32[]{:S(2)}) copy-start(f32[3,128]{1,0:T(4,128)} %param.19) | copy-start | bytes 4612
  539.6 3.7 copy-start.63
  539.6 3.7 copy-start.64
  543.3 1.6 copy-start.66
  544.0 1.5 copy-start.67
  544.0 1.7 copy-start.68
  545.5 1.6 copy-start.72
  546.3 1.4 copy-start.73
  546.3 1.7 copy-start.74
  547.7 1.6 copy-start.76
  548.7 1.4 copy-start.77
  548.7 1.7 copy-start.78
  550.0 1.6 copy-start.82
  551.0 1.4 copy-start.83
  551.0 1.7 copy-start.84
  552.3 1.7 copy-start.79
  552.3 2.0 copy-start.80
  553.6 1.4 copy-start.85
  553.6 1.7 copy-start.86
  554.9 1.7 copy-start.88
  556.0 1.4 copy-start.89
  556.0 1.7 copy-start.90
  557.2 1.6 copy-start.96
  558.3 1.5 copy-start.97
  558.3 1.8 copy-start.98
  559.5 1.4 copy-start.49
  559.5 1.7 copy-start.50
  560.8 1.7 copy-start.94
  561.9 1.5 copy-start.91
  561.9 1.7 copy-start.92
  563.3 1.6 copy-start.70
  564.2 1.4 copy-start.61
  564.2 1.7 copy-start.62
  565.6 1.6 copy-start.60
  566.6 1.4 copy-start.57
  566.6 1.7 copy-start.58
  567.9 1.7 copy-start.56
  569.1 1.7 copy-start.54
  570.2 1.4 copy-start.51
  570.2 1.7 copy-start.52
  571.4 1.4 copy-start.47
  571.4 1.7 copy-start.48
  572.5 1.4 copy-start.45
  572.5 1.7 copy-start.46
  573.8 1.7 copy-start.44
  574.9 1.4 copy-start.41
  574.9 1.7 copy-start.42
  576.1 1.4 copy-start.39
  576.1 1.7 copy-start.40
  577.2 1.4 copy-start.37
  577.2 1.7 copy-start.38
  579.5 2.3 copy-start.35
  579.5 2.3 copy-start.36
  589.1 29.3 %copy-start.1 = (s32[2,256]{1,0:T(2,128)S(1)}, s32[2,256]{1,0:T(2,128)}, u32[]{:S(2)}) copy-start(s32[2,256]{1,0:T(2,128)} %param.18) | copy-start | bytes 6148
  (38 other events, 48.5 us)
Sparse Core Ops, SparseCore 0:
  82.2 62.9 reduce-scatter.1
  147.6 37.1 all-gather.2
  537.7 35.4 all-gather.4
where the time goes:
time: 633 us; the launch traced here: 625 us
  other arithmetic  451 us (71%)
  blocking collectives  95.5 us (15%)
  local copies, waits for them, and re-layouts  36 us (6%)
  matrix products  28.3 us (4%)
  between operations  13.9 us (2%)
    another operation x20, other arithmetic  384 us
    scatter-add x2, other arithmetic, per_device(): charge_zero.at[:, local_ends[0]].add(cur_wide).at[:, local_ends[1]]  61.2 us
    dot_general x48, matrix products, apply_tile(): lax.dot_general(left, stacked, (((1,), (1,)), ((), ())), preferred_elemen...  28.3 us
    all_gather x1, blocking collectives, per_device(): sdir = lax.all_gather(src_dir, 'row', axis=1, tiled=True)  26.2 us
    all_gather x1, blocking collectives, per_device(): spos = lax.all_gather(src_pos, 'row', axis=1, tiled=True)  22.9 us
    all_gather x1, blocking collectives, per_device(): ppos = lax.all_gather(pan_pos, 'row', axis=1, tiled=True)  20.3 us
    unnamed x198, local copies, waits for them, and re-layouts  18 us
    all_gather x1, blocking collectives, per_device(): potential = lax.all_gather(potential_part, 'row', axis=1, tiled=True)  18 us
  transfers between devices with their start and end apart: 3, of which 0 were waited for; matrix products, arithmetic and copies ran while one was open for 66% of the time, Pallas kernels for 0%

commit v1 on v0

v1 whole, which is shorter than its diff:
```python
import functools
import math

import jax
import jax.numpy as jnp
from jax import lax
from jax.experimental import pallas as pl
from jax.experimental.pallas import tpu as pltpu
from jax.sharding import PartitionSpec as P

CELLS = 131072
PANELS = 65536

soft_sq = 0.0004
wave_num = 12.0
turn = wave_num / (2 * math.pi)

A1, A0, K1 = -2.24750753, 1.37545559, 2.2830122
B2, B1, B0 = -3.52005613, 4.32182737, -0.87613445
ENTRY = 2 * K1 * K1
MAGIC = 12582912.0

F32 = jnp.float32
BF16 = jnp.bfloat16


def split3(x):
    a = lax.reduce_precision(x, 8, 7)
    b = lax.reduce_precision(x - a, 8, 7)
    c = lax.reduce_precision(x - a - b, 8, 7)
    return a, b, c


def point_features(pos, is_target):
    x = (pos - 0.5) * turn
    sq = jnp.sum(x * x, axis=0, keepdims=True)
    if is_target:
        sq = sq + soft_sq * turn * turn
        x = -2.0 * x
    a, b, c = split3(x)
    n = split3(sq)
    one = jnp.ones((3, pos.shape[1]), F32)
    pad = jnp.zeros((8, pos.shape[1]), F32)
    if is_target:
        rows = [a, a, a, b, b, c, *n, one, pad]
    else:
        rows = [a, b, c, a, b, a, one, *n, pad]
    return jnp.concatenate(rows, 0).astype(BF16)


def vector_features(vec, is_target):
    a, b, c = split3(vec)
    pad = jnp.zeros((14, vec.shape[1]), F32)
    rows = [a, a, a, b, b, c, pad] if is_target else [a, b, c, a, b, a, pad]
    return jnp.concatenate(rows, 0).astype(BF16)


def entries(dist, weight):
    inverse = lax.rsqrt(dist)
    phase = dist * inverse
    f = phase - ((phase + MAGIC) - MAGIC)
    z = f * f
    s = ((z + A1) * z + A0) * f
    c = ((z + B2) * z + B1) * z + B0
    m = inverse if weight is None else inverse * weight
    real_part = (1.0 / ENTRY - s * s) * m
    imag_part = (s * m) * c
    return real_part.astype(BF16), imag_part.astype(BF16)


def dot(a, b, da, db):
    return lax.dot_general(a, b, (((da,), (db,)), ((), ())), preferred_element_type=F32)


def sweep_kernel(tb, sb, unroll, with_dir, *refs):
    if with_dir:
        ft, fs, gt, gs, wr, wi, out = refs
    else:
        ft, fs, wr, wi, out = refs
    targets = ft.shape[1]
    sources = fs.shape[0]

    @pl.loop(0, targets // tb)
    def _(t):
        tcol = pl.ds(pl.multiple_of(t * tb, tb), tb)
        fcol = ft[:, tcol]
        gcol = gt[:, tcol] if with_dir else None

        def step(j, acc):
            for u in range(unroll):
                start = pl.multiple_of((j * unroll + u) * sb, sb)
                rows = pl.ds(start, sb)
                dist = dot(fs[rows, :], fcol, 1, 0)
                weight = dot(gs[rows, :], gcol, 1, 0) if with_dir else None
                re, im = entries(dist, weight)
                acc = acc + dot(wr[:, rows], re, 1, 0) + dot(wi[:, rows], im, 1, 0)
            return acc

        out[:, tcol] = lax.fori_loop(
            0, sources // (sb * unroll), step, jnp.zeros((wr.shape[0], tb), F32)
        )


def sweep(ft, fs, gt, gs, source, tb=256, sb=256, unroll=2):
    half = source.shape[0] // 2
    targets, sources = ft.shape[1], fs.shape[0]
    tb, sb = min(tb, targets), min(sb, sources)
    unroll = min(unroll, sources // sb)
    wi = jnp.concatenate([-0.5 * source[half:], 0.5 * source[:half]], 0)
    args = (ft, fs, source, wi) if gt is None else (ft, fs, gt, gs, source, wi)
    total = targets * sources
    out = pl.pallas_call(
        functools.partial(sweep_kernel, tb, sb, unroll, gt is not None),
        out_shape=jax.ShapeDtypeStruct((source.shape[0], targets), F32),
        in_specs=[pl.BlockSpec(memory_space=pltpu.VMEM)] * len(args),
        out_specs=pl.BlockSpec(memory_space=pltpu.VMEM),
        compiler_params=pltpu.CompilerParams(vmem_limit_bytes=40 * 2**20),
        cost_estimate=pl.CostEstimate(
            flops=total * 1600, bytes_accessed=4 * 2**20, transcendentals=total
        ),
        name="sweep_cells" if gt is not None else "sweep_panels",
    )(*args)
    return out * (ENTRY * turn)


def spread_kernel(ends, cur, out):
    doubled = cur.shape[0]
    lows = out.shape[1]
    highs = out.shape[0] // doubled
    n = ends.shape[1]
    chunk = min(n, 512)

    def step(j, acc):
        cols = pl.ds(pl.multiple_of(j * chunk, chunk), chunk)
        for e in range(2):
            idx = ends[e : e + 1, cols]
            hi = idx // lows
            lo = idx - hi * lows
            hit = lax.broadcasted_iota(jnp.int32, (highs, chunk), 0) == hi
            low = jnp.where(
                lax.broadcasted_iota(jnp.int32, (lows, chunk), 0) == lo, 1.0 - 2.0 * e, 0.0
            ).astype(BF16)
            rows = [jnp.where(hit, cur[r : r + 1, cols], 0.0) for r in range(doubled)]
            acc = acc + dot(jnp.concatenate(rows, 0).astype(BF16), low, 1, 1)
        return acc

    out[...] = lax.fori_loop(0, n // chunk, step, jnp.zeros(out.shape, F32))


def spread(ends, cur_wide, block_len):
    doubled = cur_wide.shape[0]
    lows = 256
    highs = block_len // lows
    out = pl.pallas_call(
        spread_kernel,
        out_shape=jax.ShapeDtypeStruct((doubled * highs, lows), F32),
        in_specs=[pl.BlockSpec(memory_space=pltpu.VMEM)] * 2,
        out_specs=pl.BlockSpec(memory_space=pltpu.VMEM),
        compiler_params=pltpu.CompilerParams(vmem_limit_bytes=40 * 2**20),
        name="spread_charges",
    )(ends, cur_wide)
    return out.reshape(doubled, block_len)


def ends_kernel(ends, pot, base, out):
    tb = 256
    panels = pot.shape[1]
    a, b, c = split3(pot[...])
    a, b, c = a.astype(BF16), b.astype(BF16), c.astype(BF16)
    pieces = jnp.concatenate([a, b, c, jnp.zeros_like(a)], 0)
    d = a.shape[0]

    @pl.loop(0, ends.shape[1] // tb)
    def _(t):
        cols = pl.ds(pl.multiple_of(t * tb, tb), tb)
        row = lax.broadcasted_iota(jnp.int32, (panels, tb), 0)
        pick = jnp.where(row == ends[0:1, cols], 1.0, 0.0) - jnp.where(
            row == ends[1:2, cols], 1.0, 0.0
        )
        got = dot(pieces, pick.astype(BF16), 1, 0)
        out[:, cols] = base[:, cols] + (got[:d] + got[d : 2 * d]) + got[2 * d : 3 * d]


def end_difference(ends, pot, base):
    return pl.pallas_call(
        ends_kernel,
        out_shape=jax.ShapeDtypeStruct(base.shape, F32),
        in_specs=[pl.BlockSpec(memory_space=pltpu.VMEM)] * 3,
        out_specs=pl.BlockSpec(memory_space=pltpu.VMEM),
        compiler_params=pltpu.CompilerParams(vmem_limit_bytes=40 * 2**20),
        name="end_difference",
    )(ends, pot, base)


def per_device(
    currents, src_pos, src_dir, cell_ends, pan_pos, tgt_pos, tgt_dir, tgt_ends, wpan_pos
):
    doubled = currents.shape[0]
    half = doubled // 2
    col_count = lax.axis_size("col")
    rows = lax.axis_size("row")
    panel_dev = pan_pos.shape[1]
    block_len = panel_dev * rows
    tdev, wdev = tgt_pos.shape[1], wpan_pos.shape[1]
    packed = jnp.concatenate(
        [tgt_pos.reshape(-1), tgt_dir.reshape(-1), wpan_pos.reshape(-1)]
    ).reshape(1, -1, 128)
    packed = lax.all_gather(packed, "row", axis=0, tiled=True).reshape(rows, -1)
    tend = lax.all_gather(tgt_ends, "row", axis=1, tiled=True)

    cur16 = currents.astype(BF16)
    cur_wide = lax.reduce_precision(currents, 8, 7)
    local_ends = cell_ends // (panel_dev * col_count) * panel_dev + cell_ends % panel_dev
    partial_value = spread(local_ends, cur_wide, block_len)
    charge = lax.psum_scatter(partial_value, "row", scatter_dimension=1, tiled=True)

    def whole(start, width):
        piece = packed[:, start : start + 3 * width].reshape(rows, 3, width)
        return piece.transpose(1, 0, 2).reshape(3, rows * width)

    tpos = whole(0, tdev)
    tdir = whole(3 * tdev, tdev)
    wpos = whole(6 * tdev, wdev)
    induct = sweep(
        point_features(tpos, True),
        point_features(src_pos, False).T,
        vector_features(tdir, True),
        vector_features(src_dir, False).T,
        cur16,
    )
    field = sweep(
        point_features(wpos, True),
        point_features(pan_pos, False).T,
        None,
        None,
        charge.astype(BF16),
    )
    pscale = 0.25 / math.sqrt(PANELS)
    lscale = 1.0 / math.sqrt(CELLS)
    potential = jnp.concatenate([field[half:], -field[:half]], 0) * pscale
    voltage = jnp.concatenate([-induct[half:], induct[:half]], 0) * lscale
    total = end_difference(tend, potential, voltage)
    return lax.psum_scatter(total, ("row", "col"), scatter_dimension=1, tiled=True)


def solution(mesh):
    return jax.shard_map(
        per_device,
        mesh=mesh,
        in_specs=(
            P(None, ("row", "col")),
            P(None, ("row", "col")),
            P(None, ("row", "col")),
            P(None, ("row", "col")),
            P(None, ("row", "col")),
            P(None, "row"),
            P(None, "row"),
            P(None, "row"),
            P(None, "row"),
        ),
        out_specs=P(None, ("row", "col")),
        check_vma=False,
    )
```

time: 633 us -> 340 us (0.54); the launches traced: 625 us -> 339 us
  other arithmetic: 451 us -> 3.47 us
  Pallas kernels: 0 us -> 140 us
  waiting for transfers between devices: 0.77 us -> 132 us
  blocking collectives: 95.5 us -> 41 us
  matrix products: 28.3 us -> 0 us
  local copies, waits for them, and re-layouts: 36 us -> 9.36 us
    another operation x20 -> x8, other arithmetic: 384 us -> 0.26 us
    pallas_call x0 -> x4, Pallas kernels: none -> 140 us  [the longest x2 123 us: sweep(): pl.pallas_call(functools.partial(sweep_kernel, tb, sb, unroll, gt is not...]
    reduce_scatter x0 -> x1, waiting for transfers between devices: none -> 132 us  [per_device(): lax.psum_scatter(total, ('row', 'col'), scatter_dimension=1, tiled=True)]
    scatter-add x2 -> x0, other arithmetic: 61.2 us -> none  [per_device(): charge_zero.at[:, local_ends[0]].add(cur_wide).at[:, local_ends[1]]]
    all_gather x4 -> x2, blocking collectives: 87.4 us -> 41 us  [the longest x1 23.4 us: per_device(): packed = lax.all_gather(packed, 'row', axis=0, tiled=True).reshape(rows, -1)]
    dot_general x48 -> x0, matrix products: 28.3 us -> none  [apply_tile(): lax.dot_general(left, stacked, (((1,), (1,)), ((), ())), preferred_elemen...]
    unnamed x198 -> x16, local copies, waits for them, and re-layouts: 18 us -> 3.22 us
    scatter-add x1 -> x0, local copies, waits for them, and re-layouts: 9.78 us -> none  [per_device(): charge_zero.at[:, local_ends[0]].add(cur_wide).at[:, local_ends[1]]]
  transfers between devices with their start and end apart: 3 -> 2, of which waited for: 0 -> 1; matrix products, arithmetic and copies ran while one was open for 66% -> 2% of each run, Pallas kernels for 0% -> 30%
where the time goes in v1:
time: 340 us; the launch traced here: 339 us
  Pallas kernels  140 us (41%)
  waiting for transfers between devices  132 us (39%)
  blocking collectives  41 us (12%)
  between operations  13.8 us (4%)
  local copies, waits for them, and re-layouts  9.36 us (3%)
  other arithmetic  3.47 us (1%)
    reduce_scatter x1, waiting for transfers between devices, per_device(): lax.psum_scatter(total, ('row', 'col'), scatter_dimension=1, tiled=True)  132 us
    pallas_call x2, Pallas kernels, sweep(): pl.pallas_call(functools.partial(sweep_kernel, tb, sb, unroll, gt is not...  123 us
    all_gather x1, blocking collectives, per_device(): packed = lax.all_gather(packed, 'row', axis=0, tiled=True).reshape(rows, -1)  23.4 us
    all_gather x1, blocking collectives, per_device(): tend = lax.all_gather(tgt_ends, 'row', axis=1, tiled=True)  17.5 us
    pallas_call x1, Pallas kernels, end_difference(): pl.pallas_call(ends_kernel, out_shape=jax.ShapeDtypeStruct(base.shape, F3...  9.7 us
    pallas_call x1, Pallas kernels, spread(): pl.pallas_call(spread_kernel, out_shape=jax.ShapeDtypeStruct((doubled * h...  7.08 us
  transfers between devices with their start and end apart: 2, of which 1 were waited for; matrix products, arithmetic and copies ran while one was open for 2% of the time, Pallas kernels for 30%

profile of v1, /device:TPU:0, one launch (start us, length us, event | category | flops | bytes accessed | tf_op | source)
XLA Modules:
  0.0 339.2 jit_solution(17573687785788369382)
XLA Ops:
  6.5 0.0 reduce-scatter.3.cloned.1.call-start
  6.5 0.9 fusion.9.ends
  7.4 1.0 fusion.23
  8.4 7.1 %spread_charges.1 = f32[1024,256]{1,0:T(8,128)S(1)} custom-call(s32[2,4096]{1,0:T(2,128)S(1)} %fusion.9.ends, f32[8,4096]{1,0:T(8,128)S(1)} %get-tuple-element.8.cur), custom_call_target="tpu_custom_call" | custom-call | tf_op jit(solution)/shard_map/spread_charges/pallas_call | solution.py:154
  15.5 1.2 reshape.211
  16.7 0.0 copy-start.3
  16.7 0.0 copy-start.5
  16.7 0.0 reduce-scatter.3.cloned.1.call-update
  16.7 0.0 copy-start.4
  16.7 0.0 reduce-scatter.5.cloned.1.call-start
  16.8 0.6 copy-done.3
  17.4 0.0 copy-done.4
  17.4 0.0 copy-done.5
  17.4 23.4 %all_gather.7 = f32[16,15,128]{2,1,0:T(8,128)S(1)} all-gather(f32[1,15,128]{2,1,0:T(8,128)S(1)} %maximum_bitcast_fusion), channel_id=1, replica_groups=mesh['row'=16,'col'=2] {'row'}, dimensions={0}, use_global_device_ids=true | all-gather | bytes 130560 | tf_op jit(solution)/shard_map/all_gather | solution.py:208
  41.0 0.0 copy-start.2
  41.1 0.7 copy-done.2
  42.0 0.0 copy-start.1
  42.1 0.7 copy-done.1
  42.8 0.1 multiply_reduce_fusion
  43.0 0.6 concatenate.45
  43.6 0.5 copy.52
  44.1 0.0 copy-start
  44.2 0.8 copy-done
  45.0 0.8 concatenate.47
  45.8 0.5 copy.53
  46.4 0.8 concatenate.46.refs_2_
  47.2 0.6 concatenate.44.refs_0_
  47.8 103.3 %sweep_cells.1 = f32[8,4096]{1,0:T(8,128)S(1)} custom-call(bf16[32,4096]{1,0:T(8,128)(2,1)S(1)} %concatenate.44.refs_0_, bf16[4096,32]{1,0:T(8,128)(2,1)S(1)} %bitcast.32, bf16[32,4096]{1,0:T(8,128)(2,1)S(1)} %concatenate.46.refs_2_, bf16[4096,32]{1,0:T(8,128)(2,1)S(1)} %bitcast.33, bf16[8,4096]{1,0:T(8,128)(2,1)S(1)} %get-tuple-element.7.refs_4_, ...), custom_call_target="tpu_custom_call" | custom-call | flops 26843545600 | bytes 4194304 | tf_op jit(solution)/shard_map/sweep_cells/pallas_call | solution.py:112
  151.2 0.4 concatenate.41
  151.6 0.3 copy.51
  151.9 0.0 copy-start.6
  151.9 0.4 concatenate.40.refs_0_
  152.3 0.3 copy-done.6
  152.6 17.5 %all_gather.6.ends = s32[2,4096]{1,0:T(2,128)S(1)} all-gather(s32[2,256]{1,0:T(2,128)S(1)} %copy-done.6), channel_id=1, replica_groups=mesh['row'=16,'col'=2] {'row'}, dimensions={1}, use_global_device_ids=true | all-gather | bytes 34816 | tf_op jit(solution)/shard_map/all_gather | solution.py:209
  170.2 0.0 reduce-scatter.3.cloned.1.call-done
  170.2 0.8 convert_element_type.4.refs_2_
  171.1 19.5 %sweep_panels.1 = f32[8,2048]{1,0:T(8,128)S(1)} custom-call(bf16[32,2048]{1,0:T(8,128)(2,1)S(1)} %concatenate.40.refs_0_, bf16[2048,32]{1,0:T(8,128)(2,1)S(1)} %bitcast.34, bf16[8,2048]{1,0:T(8,128)(2,1)S(1)} %convert_element_type.4.refs_2_, bf16[8,2048]{1,0:T(8,128)(2,1)S(1)} %pad_maximum_fusion.1.refs_3_), custom_call_target="tpu_custom_call" | custom-call | flops 6710886400 | bytes 4194304 | tf_op jit(solution)/shard_map/sweep_panels/pallas_call | solution.py:112
  190.7 9.7 %end_difference.1 = f32[8,4096]{1,0:T(8,128)} custom-call(s32[2,4096]{1,0:T(2,128)S(1)} %all_gather.6.ends, f32[8,2048]{1,0:T(8,128)S(1)} %maximum_multiply_fusion.1.pot, f32[8,4096]{1,0:T(8,128)S(1)} %maximum_multiply_fusion.base), custom_call_target="tpu_custom_call" | custom-call | tf_op jit(solution)/shard_map/end_difference/pallas_call | solution.py:185
  200.4 0.0 reduce-scatter.5.cloned.1.call-update
  200.5 131.9 %reduce-scatter.5.cloned.1.call-done = f32[8,128]{1,0:T(8,128)} async-done(((f32[8,4096]{1,0:T(8,128)}), f32[8,128]{1,0:T(8,128)}) %reduce-scatter.5.cloned.1.call-update) | async-done | bytes 4112 | tf_op jit(solution)/shard_map/reduce_scatter | solution.py:243
  (40 shorter events, 0.9 us)
Async XLA Ops:
  6.5 163.7 %reduce-scatter.3.cloned.1.call-start = ((), (), s32[]{:S(2)}) async-start(), calls=%async_computation.2 | async-start | bytes 1114112 | tf_op jit(solution)/shard_map/reduce_scatter | solution.py:215
  16.7 0.7 copy-start.3
  16.7 0.7 copy-start.5
  16.7 0.7 copy-start.4
  16.7 315.7 %reduce-scatter.5.cloned.1.call-start = ((), (), s32[]{:S(2)}) async-start(), calls=%async_computation.3 | async-start | bytes 135168 | tf_op jit(solution)/shard_map/reduce_scatter | solution.py:243
  41.0 0.8 copy-start.2
  42.0 0.8 copy-start.1
  44.1 0.8 copy-start
  151.9 0.7 copy-start.6
Sparse Core Ops, SparseCore 0:
  16.8 60.2 reduce-scatter.2
  200.6 131.7 reduce-scatter.4

commit v2 on v1

--- a/solution.py
+++ b/solution.py
@@ -101,7 +101,7 @@
         )
 
 
-def sweep(ft, fs, gt, gs, source, tb=256, sb=256, unroll=2):
+def sweep(ft, fs, gt, gs, source, tb=1024, sb=128, unroll=2):
     half = source.shape[0] // 2
     targets, sources = ft.shape[1], fs.shape[0]
     tb, sb = min(tb, targets), min(sb, sources)
@@ -192,6 +192,82 @@
     )(ends, pot, base)
 
 
+def exchange_kernel(axes, add, src, out, recv, send_sem, recv_sem):
+    count = recv.shape[0]
+    me = lax.axis_index(axes)
+    cols = lax.axis_size("col")
+    my_col = lax.axis_index("col")
+
+    def device(k):
+        other = lax.rem(me + k, count)
+        if len(axes) == 1:
+            return other, (other, my_col)
+        return other, (other // cols, lax.rem(other, cols))
+
+    def copy(k):
+        other, place = device(k)
+        return pltpu.make_async_remote_copy(
+            src_ref=src.at[other] if add else src,
+            dst_ref=recv.at[k],
+            send_sem=send_sem.at[k],
+            recv_sem=recv_sem.at[k],
+            device_id=place,
+            device_id_type=pl.DeviceIdType.MESH,
+        )
+
+    barrier = pltpu.get_barrier_semaphore()
+
+    def greet(k, carry):
+        pl.semaphore_signal(
+            barrier, inc=1, device_id=device(k)[1], device_id_type=pl.DeviceIdType.MESH
+        )
+        return carry
+
+    lax.fori_loop(1, count, greet, 0)
+    pl.semaphore_wait(barrier, count - 1)
+
+    def start(k, carry):
+        copy(k).start()
+        return carry
+
+    lax.fori_loop(1, count, start, 0)
+    if add:
+
+        def finish(k, total):
+            copy(k).wait()
+            return total + recv[k]
+
+        out[...] = lax.fori_loop(1, count, finish, src[me])
+    else:
+        out[me] = src[...]
+
+        def finish(k, carry):
+            copy(k).wait()
+            out[lax.rem(me + count - k, count)] = recv[k]
+            return carry
+
+        lax.fori_loop(1, count, finish, 0)
+
+
+def exchange(x, axes, count, add, number):
+    block = x.shape[1:] if add else x.shape
+    return pl.pallas_call(
+        functools.partial(exchange_kernel, axes, add),
+        out_shape=jax.ShapeDtypeStruct(block if add else (count, *block), x.dtype),
+        in_specs=[pl.BlockSpec(memory_space=pltpu.VMEM)],
+        out_specs=pl.BlockSpec(memory_space=pltpu.VMEM),
+        scratch_shapes=[
+            pltpu.VMEM((count, *block), x.dtype),
+            pltpu.SemaphoreType.DMA((count,)),
+            pltpu.SemaphoreType.DMA((count,)),
+        ],
+        compiler_params=pltpu.CompilerParams(
+            collective_id=number, has_side_effects=True, vmem_limit_bytes=24 * 2**20
+        ),
+        name="exchange_sum" if add else "exchange_gather",
+    )(x)
+
+
 def per_device(
     currents, src_pos, src_dir, cell_ends, pan_pos, tgt_pos, tgt_dir, tgt_ends, wpan_pos
 ):
@@ -203,10 +279,14 @@
     block_len = panel_dev * rows
     tdev, wdev = tgt_pos.shape[1], wpan_pos.shape[1]
     packed = jnp.concatenate(
-        [tgt_pos.reshape(-1), tgt_dir.reshape(-1), wpan_pos.reshape(-1)]
-    ).reshape(1, -1, 128)
-    packed = lax.all_gather(packed, "row", axis=0, tiled=True).reshape(rows, -1)
-    tend = lax.all_gather(tgt_ends, "row", axis=1, tiled=True)
+        [
+            tgt_pos.reshape(-1),
+            tgt_dir.reshape(-1),
+            wpan_pos.reshape(-1),
+            tgt_ends.astype(F32).reshape(-1),
+        ]
+    ).reshape(-1, 128)
+    packed = exchange(packed, ("row",), rows, False, 0).reshape(rows, -1)
 
     cur16 = currents.astype(BF16)
     cur_wide = lax.reduce_precision(currents, 8, 7)
@@ -214,13 +294,14 @@
     partial_value = spread(local_ends, cur_wide, block_len)
     charge = lax.psum_scatter(partial_value, "row", scatter_dimension=1, tiled=True)
 
-    def whole(start, width):
-        piece = packed[:, start : start + 3 * width].reshape(rows, 3, width)
-        return piece.transpose(1, 0, 2).reshape(3, rows * width)
+    def whole(start, width, dims=3):
+        piece = packed[:, start : start + dims * width].reshape(rows, dims, width)
+        return piece.transpose(1, 0, 2).reshape(dims, rows * width)
 
     tpos = whole(0, tdev)
     tdir = whole(3 * tdev, tdev)
     wpos = whole(6 * tdev, wdev)
+    tend = whole(6 * tdev + 3 * wdev, tdev, 2).astype(jnp.int32)
     induct = sweep(
         point_features(tpos, True),
         point_features(src_pos, False).T,
@@ -240,7 +321,9 @@
     potential = jnp.concatenate([field[half:], -field[:half]], 0) * pscale
     voltage = jnp.concatenate([-induct[half:], induct[:half]], 0) * lscale
     total = end_difference(tend, potential, voltage)
-    return lax.psum_scatter(total, ("row", "col"), scatter_dimension=1, tiled=True)
+    count = rows * col_count
+    blocks = total.reshape(doubled, count, -1).transpose(1, 0, 2)
+    return exchange(blocks, ("row", "col"), count, True, 1)
 
 
 def solution(mesh):

time: 340 us -> 163 us (0.48)
  waiting for transfers between devices: 132 us -> 0.04 us
  blocking collectives: 41 us -> 0 us
  Pallas kernels: 140 us -> 133 us
    reduce_scatter x1 -> x0, waiting for transfers between devices: 132 us -> none  [per_device(): lax.psum_scatter(total, ('row', 'col'), scatter_dimension=1, tiled=True)]
    all_gather x2 -> x0, blocking collectives: 41 us -> none  [the longest x1 23.4 us: per_device(): packed = lax.all_gather(packed, 'row', axis=0, tiled=True).reshape(rows, -1)]
    pallas_call x2, Pallas kernels: 123 us -> 97.2 us  [sweep(): pl.pallas_call(functools.partial(sweep_kernel, tb, sb, unroll, gt is not...]
    pallas_call x0 -> x2, Pallas kernels: none -> 19.7 us  [exchange(): pl.pallas_call(functools.partial(exchange_kernel, axes, add), out_shape=j...]
  transfers between devices with their start and end apart: 2 -> 1, of which waited for: 1 -> 0; matrix products, arithmetic and copies ran while one was open for 2% -> 4% of each run, Pallas kernels for 30% -> 55%
where the time goes in v2:
time: 163 us; the launch traced here: 162 us
  Pallas kernels  133 us (82%)
  between operations  13.8 us (8%)
  local copies, waits for them, and re-layouts  11.8 us (7%)
  other arithmetic  3.48 us (2%)
    pallas_call x2, Pallas kernels, sweep(): pl.pallas_call(functools.partial(sweep_kernel, tb, sb, unroll, gt is not...  97.2 us
    pallas_call x2, Pallas kernels, exchange(): pl.pallas_call(functools.partial(exchange_kernel, axes, add), out_shape=j...  19.7 us
    pallas_call x1, Pallas kernels, end_difference(): pl.pallas_call(ends_kernel, out_shape=jax.ShapeDtypeStruct(base.shape, F3...  9.05 us
    pallas_call x1, Pallas kernels, spread(): pl.pallas_call(spread_kernel, out_shape=jax.ShapeDtypeStruct((doubled * h...  7.08 us
    unnamed x18, local copies, waits for them, and re-layouts  5.6 us
  transfers between devices with their start and end apart: 1, of which 0 were waited for; matrix products, arithmetic and copies ran while one was open for 4% of the time, Pallas kernels for 55%

profile of v2, /device:TPU:0, one launch (start us, length us, event | category | flops | bytes accessed | tf_op | source)
XLA Modules:
  0.0 162.0 jit_solution(6380485496430762550)
XLA Ops:
  6.5 0.0 reduce-scatter.2.cloned.1.call-start
  6.5 0.9 fusion.9.ends
  7.4 1.0 fusion.24
  8.4 7.1 %spread_charges.1 = f32[1024,256]{1,0:T(8,128)S(1)} custom-call(s32[2,4096]{1,0:T(2,128)S(1)} %fusion.9.ends, f32[8,4096]{1,0:T(8,128)S(1)} %get-tuple-element.13.cur), custom_call_target="tpu_custom_call" | custom-call | tf_op jit(solution)/shard_map/spread_charges/pallas_call | solution.py:154
  15.5 1.2 reshape.222
  16.7 0.0 copy-start.6
  16.7 0.0 reduce-scatter.2.cloned.1.call-update
  16.7 0.7 copy-done.6
  17.3 0.0 copy-start.3
  17.4 0.7 copy-done.3
  18.0 0.0 copy-start.4
  18.0 0.7 copy-done.4
  18.7 0.0 copy-start.5
  18.7 0.7 copy-done.5
  19.4 9.9 %exchange_gather.1 = f32[16,19,128]{2,1,0:T(8,128)S(1)} custom-call(f32[19,128]{1,0:T(8,128)S(1)} %maximum_bitcast_fusion.src), custom_call_target="tpu_custom_call" | custom-call | tf_op jit(solution)/shard_map/exchange_gather/pallas_call | solution.py:254
  29.5 0.0 copy-start.2
  29.5 0.7 copy-done.2
  30.5 0.0 copy-start.1
  30.6 0.8 copy-done.1
  31.3 0.1 multiply_reduce_fusion
  31.5 0.6 concatenate.45
  32.1 0.5 copy.52
  32.6 0.0 copy-start
  32.7 0.8 copy-done
  33.5 0.8 concatenate.47
  34.3 0.5 copy.53
  34.9 0.8 concatenate.46.refs_2_
  35.7 0.6 concatenate.44.refs_0_
  36.3 79.3 %sweep_cells.1 = f32[8,4096]{1,0:T(8,128)S(1)} custom-call(bf16[32,4096]{1,0:T(8,128)(2,1)S(1)} %concatenate.44.refs_0_, bf16[4096,32]{1,0:T(8,128)(2,1)S(1)} %bitcast.41, bf16[32,4096]{1,0:T(8,128)(2,1)S(1)} %concatenate.46.refs_2_, bf16[4096,32]{1,0:T(8,128)(2,1)S(1)} %bitcast.42, bf16[8,4096]{1,0:T(8,128)(2,1)S(1)} %get-tuple-element.12.refs_4_, ...), custom_call_target="tpu_custom_call" | custom-call | flops 26843545600 | bytes 4194304 | tf_op jit(solution)/shard_map/sweep_cells/pallas_call | solution.py:112
  115.7 0.4 concatenate.41
  116.1 0.3 copy.51
  116.3 0.4 concatenate.40.refs_0_
  116.8 0.0 reduce-scatter.2.cloned.1.call-done
  116.8 0.8 convert_element_type.29.refs_2_
  117.8 17.9 %sweep_panels.1 = f32[8,2048]{1,0:T(8,128)S(1)} custom-call(bf16[32,2048]{1,0:T(8,128)(2,1)S(1)} %concatenate.40.refs_0_, bf16[2048,32]{1,0:T(8,128)(2,1)S(1)} %bitcast.44, bf16[8,2048]{1,0:T(8,128)(2,1)S(1)} %convert_element_type.29.refs_2_, bf16[8,2048]{1,0:T(8,128)(2,1)S(1)} %pad_maximum_fusion.1.refs_3_), custom_call_target="tpu_custom_call" | custom-call | flops 6710886400 | bytes 4194304 | tf_op jit(solution)/shard_map/sweep_panels/pallas_call | solution.py:112
  135.7 9.0 %end_difference.1 = f32[8,4096]{1,0:T(8,128)S(1)} custom-call(s32[2,4096]{1,0:T(2,128)S(1)} %bitcast.46, f32[8,2048]{1,0:T(8,128)S(1)} %maximum_multiply_fusion.1.pot, f32[8,4096]{1,0:T(8,128)S(1)} %maximum_multiply_fusion.base), custom_call_target="tpu_custom_call" | custom-call | tf_op jit(solution)/shard_map/end_difference/pallas_call | solution.py:185
  144.8 9.8 %exchange_sum.1 = f32[8,128]{1,0:T(8,128)S(1)} custom-call(f32[32,8,128]{2,1,0:T(8,128)S(1)} %bitcast.45), custom_call_target="tpu_custom_call" | custom-call | tf_op jit(solution)/shard_map/exchange_sum/pallas_call | solution.py:254
  154.6 0.6 copy.60
  (44 shorter events, 0.9 us)
Async XLA Ops:
  6.5 110.3 %reduce-scatter.2.cloned.1.call-start = ((), (), s32[]{:S(2)}) async-start(), calls=%async_computation.1 | async-start | bytes 1114112 | tf_op jit(solution)/shard_map/reduce_scatter | solution.py:295
  16.7 0.7 copy-start.6
  17.3 0.7 copy-start.3
  18.0 0.7 copy-start.4
  18.7 0.7 copy-start.5
  29.5 0.8 copy-start.2
  30.5 0.8 copy-start.1
  32.6 0.8 copy-start
Sparse Core Ops, SparseCore 0:
  16.8 60.1 reduce-scatter.1

commit v3 on v2

--- a/solution.py
+++ b/solution.py
@@ -101,7 +101,7 @@
         )
 
 
-def sweep(ft, fs, gt, gs, source, tb=1024, sb=128, unroll=2):
+def sweep(ft, fs, gt, gs, source, tb=1024, sb=256, unroll=2):
     half = source.shape[0] // 2
     targets, sources = ft.shape[1], fs.shape[0]
     tb, sb = min(tb, targets), min(sb, sources)
@@ -174,8 +174,8 @@
     def _(t):
         cols = pl.ds(pl.multiple_of(t * tb, tb), tb)
         row = lax.broadcasted_iota(jnp.int32, (panels, tb), 0)
-        pick = jnp.where(row == ends[0:1, cols], 1.0, 0.0) - jnp.where(
-            row == ends[1:2, cols], 1.0, 0.0
+        pick = jnp.where(
+            row == ends[0:1, cols], 1.0, jnp.where(row == ends[1:2, cols], -1.0, 0.0)
         )
         got = dot(pieces, pick.astype(BF16), 1, 0)
         out[:, cols] = base[:, cols] + (got[:d] + got[d : 2 * d]) + got[2 * d : 3 * d]

time: 163 us -> 147 us (0.902)
  Pallas kernels: 133 us -> 118 us
    pallas_call x2, Pallas kernels: 97.2 us -> 83 us  [sweep(): pl.pallas_call(functools.partial(sweep_kernel, tb, sb, unroll, gt is not...]
  transfers between devices with their start and end apart: 1 -> 1, of which waited for: 0 -> 0; matrix products, arithmetic and copies ran while one was open for 4% -> 4% of each run, Pallas kernels for 55% -> 53%
where the time goes in v3:
time: 147 us
  Pallas kernels  118 us (80%)
  between operations  13.8 us (9%)
  local copies, waits for them, and re-layouts  11.8 us (8%)
  other arithmetic  3.48 us (2%)
    pallas_call x2, Pallas kernels, sweep(): pl.pallas_call(functools.partial(sweep_kernel, tb, sb, unroll, gt is not...  83 us
    pallas_call x2, Pallas kernels, exchange(): pl.pallas_call(functools.partial(exchange_kernel, axes, add), out_shape=j...  19.7 us
    pallas_call x1, Pallas kernels, end_difference(): pl.pallas_call(ends_kernel, out_shape=jax.ShapeDtypeStruct(base.shape, F3...  7.96 us
    pallas_call x1, Pallas kernels, spread(): pl.pallas_call(spread_kernel, out_shape=jax.ShapeDtypeStruct((doubled * h...  7.08 us
    unnamed x18, local copies, waits for them, and re-layouts  5.6 us
  transfers between devices with their start and end apart: 1, of which 0 were waited for; matrix products, arithmetic and copies ran while one was open for 4% of the time, Pallas kernels for 53%

profile of v3, /device:TPU:0, one launch (start us, length us, event | category | flops | bytes accessed | tf_op | source)
XLA Modules:
  0.0 146.7 jit_solution(1205683920019405863)
XLA Ops:
  6.5 0.0 reduce-scatter.2.cloned.1.call-start
  6.5 0.9 fusion.9.ends
  7.4 1.0 fusion.24
  8.4 7.1 %spread_charges.1 = f32[1024,256]{1,0:T(8,128)S(1)} custom-call(s32[2,4096]{1,0:T(2,128)S(1)} %fusion.9.ends, f32[8,4096]{1,0:T(8,128)S(1)} %get-tuple-element.13.cur), custom_call_target="tpu_custom_call" | custom-call | tf_op jit(solution)/shard_map/spread_charges/pallas_call | solution.py:154
  15.5 1.2 reshape.222
  16.7 0.0 copy-start.6
  16.7 0.0 reduce-scatter.2.cloned.1.call-update
  16.7 0.7 copy-done.6
  17.3 0.0 copy-start.3
  17.4 0.7 copy-done.3
  18.0 0.0 copy-start.4
  18.0 0.7 copy-done.4
  18.7 0.0 copy-start.5
  18.7 0.7 copy-done.5
  19.4 9.9 %exchange_gather.1 = f32[16,19,128]{2,1,0:T(8,128)S(1)} custom-call(f32[19,128]{1,0:T(8,128)S(1)} %maximum_bitcast_fusion.src), custom_call_target="tpu_custom_call" | custom-call | tf_op jit(solution)/shard_map/exchange_gather/pallas_call | solution.py:254
  29.5 0.0 copy-start.2
  29.5 0.7 copy-done.2
  30.5 0.0 copy-start.1
  30.6 0.8 copy-done.1
  31.3 0.1 multiply_reduce_fusion
  31.5 0.6 concatenate.45
  32.1 0.5 copy.52
  32.6 0.0 copy-start
  32.7 0.8 copy-done
  33.5 0.8 concatenate.47
  34.3 0.5 copy.53
  34.9 0.8 concatenate.46.refs_2_
  35.7 0.6 concatenate.44.refs_0_
  36.3 68.2 %sweep_cells.1 = f32[8,4096]{1,0:T(8,128)S(1)} custom-call(bf16[32,4096]{1,0:T(8,128)(2,1)S(1)} %concatenate.44.refs_0_, bf16[4096,32]{1,0:T(8,128)(2,1)S(1)} %bitcast.41, bf16[32,4096]{1,0:T(8,128)(2,1)S(1)} %concatenate.46.refs_2_, bf16[4096,32]{1,0:T(8,128)(2,1)S(1)} %bitcast.42, bf16[8,4096]{1,0:T(8,128)(2,1)S(1)} %get-tuple-element.12.refs_4_, ...), custom_call_target="tpu_custom_call" | custom-call | flops 26843545600 | bytes 4194304 | tf_op jit(solution)/shard_map/sweep_cells/pallas_call | solution.py:112
  104.6 0.4 concatenate.41
  105.0 0.3 copy.51
  105.3 0.4 concatenate.40.refs_0_
  105.8 0.0 reduce-scatter.2.cloned.1.call-done
  105.8 0.8 convert_element_type.29.refs_2_
  106.7 14.8 %sweep_panels.1 = f32[8,2048]{1,0:T(8,128)S(1)} custom-call(bf16[32,2048]{1,0:T(8,128)(2,1)S(1)} %concatenate.40.refs_0_, bf16[2048,32]{1,0:T(8,128)(2,1)S(1)} %bitcast.44, bf16[8,2048]{1,0:T(8,128)(2,1)S(1)} %convert_element_type.29.refs_2_, bf16[8,2048]{1,0:T(8,128)(2,1)S(1)} %pad_maximum_fusion.1.refs_3_), custom_call_target="tpu_custom_call" | custom-call | flops 6710886400 | bytes 4194304 | tf_op jit(solution)/shard_map/sweep_panels/pallas_call | solution.py:112
  121.5 8.0 %end_difference.1 = f32[8,4096]{1,0:T(8,128)S(1)} custom-call(s32[2,4096]{1,0:T(2,128)S(1)} %bitcast.46, f32[8,2048]{1,0:T(8,128)S(1)} %maximum_multiply_fusion.1.pot, f32[8,4096]{1,0:T(8,128)S(1)} %maximum_multiply_fusion.base), custom_call_target="tpu_custom_call" | custom-call | tf_op jit(solution)/shard_map/end_difference/pallas_call | solution.py:185
  129.5 9.8 %exchange_sum.1 = f32[8,128]{1,0:T(8,128)S(1)} custom-call(f32[32,8,128]{2,1,0:T(8,128)S(1)} %bitcast.45), custom_call_target="tpu_custom_call" | custom-call | tf_op jit(solution)/shard_map/exchange_sum/pallas_call | solution.py:254
  139.3 0.6 copy.60
  (44 shorter events, 0.9 us)
Async XLA Ops:
  6.5 99.3 %reduce-scatter.2.cloned.1.call-start = ((), (), s32[]{:S(2)}) async-start(), calls=%async_computation.1 | async-start | bytes 1114112 | tf_op jit(solution)/shard_map/reduce_scatter | solution.py:295
  16.7 0.7 copy-start.6
  17.3 0.7 copy-start.3
  18.0 0.7 copy-start.4
  18.7 0.7 copy-start.5
  29.5 0.8 copy-start.2
  30.5 0.8 copy-start.1
  32.6 0.8 copy-start
Sparse Core Ops, SparseCore 0:
  16.8 60.1 reduce-scatter.1
